TPU v7x, 32 devices: a whole 2x2x4 slice. The times are simulated.
32 devices in a mesh: groups: 2 (over x), vocab: 16 (over z, y, core).
Axes of the slice: x: 2, y: 2, z: 4, core: 2. Of those that a mesh axis runs over, the one named last changes fastest.
Arguments:
- hidden: bfloat16 [256, 8192], P('groups'), parts along dimension 0, may hold values from -312 to 312
- student_weight: bfloat16 [8192, 8192], P(None, 'vocab'), may hold values from -0.0625 to 0.0625
- teacher_codes: bfloat16 [16384, 256], P('vocab', 'groups'), parts along dimension 1, may hold values from -12 to 120
- teacher_exps: int32 [512, 256], P('vocab', 'groups'), parts along dimension 1, may hold values from -2 to 1
- pair_tile: int32 [384], P('vocab'), may hold values from 0 to 7
- pair_dest: int32 [384, 1], P('vocab'), may hold values from 0 to 15; in each aligned block of 24 rows (0 to 23, 24 to 47, ...) at most 2 rows name the same one
- pair_block: int32 [384], P('vocab'), may hold values from 0 to 3
- pair_map: int32 [384, 128], P('vocab'), may hold values from 0 to 159
Outputs:
- grad_hidden: bfloat16 [8192, 256], P('vocab', 'groups'), parts along dimension 1
There are 2 independent parts, one for each index of `groups`. A program takes and returns all parts, laid end to end along the dimension named above; an argument that names none is the same for every part. Nothing has to cross between parts.
Inputs may be any that keep to these rules, and one draw needn't show every extreme that they name: `pair_dest`: each aligned block of 24 rows is one vocab index's list; in it no owner is named more than 2 times, a bound that some block reaches. `pair_map`: entries of 128 or more join the teacher entry to no student entry.
All inputs are finite; a program needn't handle non-finite values.
Results may differ from a plain program's by a relative error of at most 0.001.
The roundings to bfloat16 on the way count: a program that leaves them out, or rounds other values in their place, can miss the bound.
Values may be sent and summed in bfloat16 or wider, within the bound.
A program may use at most 128 MiB of HBM per device.

v0:
```python
import jax
import jax.numpy as jnp
from jax import lax
from jax.sharding import PartitionSpec as P

BLK = 128
CAP = 2


smoothing = 0.05
loss_scale = 64.0
group_size = 16


def merged(value, axis, join):
    pieces = jax.tree.map(lambda part: lax.all_gather(part, axis), value)
    head = jax.tree.map(lambda part: part[0], pieces)
    tail = jax.tree.map(lambda part: part[1:], pieces)
    running, _ = lax.scan(lambda running, piece: (join(running, piece), None), head, tail)
    return running


def merge_partial(earlier, later):
    maximum = jnp.maximum(earlier[0], later[0])
    totals = earlier[1] * jnp.exp(earlier[0] - maximum) + later[1] * jnp.exp(later[0] - maximum)
    return (maximum, totals)


def column_partials(values):
    maximum = jnp.max(values, axis=0)
    totals = jnp.sum(jnp.exp(values - maximum[None, :]), axis=0)
    return (maximum, totals)


def decode_logits(codes_part, exps_part):
    scales = jnp.exp2(jnp.repeat(exps_part.astype(jnp.float32), 32, axis=-2))
    return codes_part.astype(jnp.float32) * scales


def slot_sources(pair_dest, owners):
    pair_count = pair_dest.shape[0]
    target = pair_dest[:, 0]
    positions = jnp.arange(pair_count, dtype=jnp.int32)
    earlier = (target[None, :] == target[:, None]) & (positions[None, :] < positions[:, None])
    earlier_count = jnp.sum(earlier.astype(jnp.int32), axis=1)
    slot_index = target * CAP + earlier_count
    places = jnp.arange(owners * CAP, dtype=jnp.int32)
    matches = (slot_index[None, :] == places[:, None]).astype(jnp.int32)
    filled = jnp.sum(matches, axis=1)
    source = jnp.sum(matches * positions[None, :], axis=1)
    return (source, filled)


def per_device(
    hidden, student_weight, teacher_codes, teacher_exps, pair_tile, pair_dest, pair_block, pair_map
):
    owners = lax.axis_size("vocab")
    vocab_local = student_weight.shape[1]
    tokens = hidden.shape[0]
    teacher_logits = decode_logits(teacher_codes, teacher_exps)
    teacher_peak, teacher_totals = column_partials(teacher_logits)
    logits_rows = lax.optimization_barrier(
        jnp.dot(hidden, student_weight, preferred_element_type=jnp.float32)
    )
    student_logits = logits_rows.T
    student_peak, student_totals = column_partials(student_logits)
    teacher_peak, teacher_totals = merged((teacher_peak, teacher_totals), "vocab", merge_partial)
    student_peak, student_totals = merged((student_peak, student_totals), "vocab", merge_partial)
    teacher_lse = teacher_peak + jnp.log(teacher_totals)
    source, filled = slot_sources(pair_dest, owners)
    slot_tiles = jnp.take(pair_tile, source)
    slot_map = jnp.where(filled[:, None] > 0, jnp.take(pair_map, source, axis=0), BLK).reshape(
        owners, CAP, BLK
    )
    slot_blocks = jnp.take(pair_block, source).reshape(owners, CAP)

    def accumulate(probabilities, map_part, block_part):
        item_count = probabilities.shape[1]
        columns = jnp.arange(vocab_local, dtype=jnp.int32)
        student_cols = jnp.where(
            map_part < BLK, block_part[..., None] * BLK + map_part, vocab_local
        )
        results = []
        for item in range(item_count):
            picker = (columns[:, None] == student_cols[:, item, :].reshape(-1)[None, :]).astype(
                jnp.bfloat16
            )
            values = probabilities[:, item].reshape(-1, tokens)
            results.append(jnp.dot(picker, values, preferred_element_type=jnp.float32))
        return jnp.stack(results, axis=0)

    send_codes = jnp.take(teacher_codes.reshape(-1, BLK, tokens), slot_tiles, axis=0).reshape(
        owners, CAP, BLK, tokens
    )
    send_exps = jnp.take(teacher_exps.reshape(-1, BLK // 32, tokens), slot_tiles, axis=0).reshape(
        owners, CAP, BLK // 32, tokens
    )

    def decode_piece(pieces):
        return jnp.exp(decode_logits(pieces[0], pieces[1]) - teacher_lse).astype(jnp.bfloat16)

    received = (
        lax.all_to_all(send_codes, "vocab", split_axis=0, concat_axis=0, tiled=True),
        lax.all_to_all(send_exps, "vocab", split_axis=0, concat_axis=0, tiled=True),
        lax.all_to_all(slot_map, "vocab", split_axis=0, concat_axis=0, tiled=True),
        lax.all_to_all(slot_blocks, "vocab", split_axis=0, concat_axis=0, tiled=True),
    )
    leading = received[0]
    item_count = leading.shape[1]
    rounds = leading.shape[0] // group_size
    stacked = tuple(
        (member.reshape((rounds, group_size) + member.shape[1:]) for member in received)
    )

    def add_round(running, pieces):
        return (running + accumulate(decode_piece(pieces), pieces[-2], pieces[-1]), None)

    start_value = jnp.zeros((item_count, vocab_local, tokens), jnp.float32)
    result, unused = lax.scan(add_round, start_value, stacked)
    mapped = result
    mapped = jnp.sum(mapped, axis=0)
    mass_totals = lax.psum(jnp.sum(mapped, axis=0), "vocab")
    vocab_total = vocab_local * owners
    target = (mapped + smoothing / vocab_total) / (mass_totals[None, :] + smoothing)
    student_lse = student_peak + jnp.log(student_totals)
    student_probs = jnp.exp(student_logits - student_lse[None, :])
    residual = (loss_scale * (student_probs - target)).astype(jnp.bfloat16)
    gradient = lax.psum_scatter(
        jnp.dot(student_weight, residual, preferred_element_type=jnp.float32),
        "vocab",
        scatter_dimension=0,
        tiled=True,
    )
    return gradient.astype(jnp.bfloat16)


def solution(mesh):
    return jax.shard_map(
        per_device,
        mesh=mesh,
        in_specs=(
            P("groups", None),
            P(None, "vocab"),
            P("vocab", "groups"),
            P("vocab", "groups"),
            P("vocab"),
            P("vocab", None),
            P("vocab"),
            P("vocab", None),
        ),
        out_specs=P("vocab", "groups"),
        check_vma=False,
    )
```

profile of v0, /device:TPU:0, one launch (start us, length us, event | category | flops | bytes accessed | tf_op | source)
XLA Modules:
  0.0 279.0 jit_solution(16527839593446086031)
XLA Ops:
  6.5 1.0 convert_reduce_fusion.1
  7.5 0.7 multiply_add_fusion
  8.3 1.4 gather_fusion.3
  9.7 0.7 all_to_all.16
  10.4 7.4 %all-to-all-start.1 = ((s32[16,1,2]{2,1,0:T(1,128)}), s32[16,1,2]{2,1,0:T(1,128)S(1)}, u32[]{:S(2)}, u32[]{:S(2)}) async-start(s32[16,1,2]{2,1,0:T(1,128)} %bitcast.13), calls=%async_computation.1 | async-start | bytes 16384 | tf_op jit(solution)/shard_map/all_to_all | solution.py:106
  17.9 0.7 multiply_exponential_fusion.1
  18.6 1.1 fusion.18
  19.7 1.1 exponential_reduce_fusion
  20.8 21.6 %all-gather.6 = f32[16,1,128]{2,1,0:T(1,128)S(1)} all-gather(f32[1,1,128]{2,1,0:T(1,128)S(1)} %bitcast.114), channel_id=4, replica_groups=mesh['groups'=2,'vocab'=16] {'vocab'}, dimensions={0}, use_global_device_ids=true | all-gather | bytes 8704 | tf_op jit(solution)/shard_map/all_gather | solution.py:16
  42.4 17.3 %all-gather.7 = f32[16,1,128]{2,1,0:T(1,128)S(1)} all-gather(f32[1,1,128]{2,1,0:T(1,128)S(1)} %bitcast.116), channel_id=5, replica_groups=mesh['groups'=2,'vocab'=16] {'vocab'}, dimensions={0}, use_global_device_ids=true | all-gather | bytes 8704 | tf_op jit(solution)/shard_map/all_gather | solution.py:16
  59.7 1.4 gather_fusion.4
  62.0 4.7 %fusion.35 = f32[128,512]{1,0:T(8,128)S(1)} fusion(bf16[128,8192]{1,0:T(8,128)(2,1)S(1)} %copy-done, bf16[8192,512]{1,0:T(8,128)(2,1)} %param.15), kind=kOutput, calls=%fused_computation.85 | convolution fusion | flops 1073741824 | bytes 10747904 | tf_op jit(solution)/shard_map/dot_general | solution.py:63
  67.0 0.6 gather_fusion.2
  67.6 1.7 gather_fusion.1
  69.3 0.7 broadcast_select_fusion.1
  70.0 2.4 broadcast_select_fusion
  73.0 0.7 select_select_fusion
  73.7 18.7 %all-gather.5 = f32[16,1,128]{2,1,0:T(1,128)S(1)} all-gather(f32[1,1,128]{2,1,0:T(1,128)S(1)} %bitcast.115), channel_id=3, replica_groups=mesh['groups'=2,'vocab'=16] {'vocab'}, dimensions={0}, use_global_device_ids=true | all-gather | bytes 8704 | tf_op jit(solution)/shard_map/all_gather | solution.py:16
  92.4 3.5 %all-to-all-start = ((s32[16,2,128]{2,1,0:T(2,128)}), s32[16,2,128]{2,1,0:T(2,128)S(1)}, u32[]{:S(2)}, u32[]{:S(2)}) async-start(s32[16,2,128]{2,1,0:T(2,128)} %select_select_fusion), calls=%async_computation | async-start | bytes 32768 | tf_op jit(solution)/shard_map/all_to_all | solution.py:105
  95.9 21.6 %all-gather.4 = f32[16,1,128]{2,1,0:T(1,128)S(1)} all-gather(f32[1,1,128]{2,1,0:T(1,128)S(1)} %bitcast.113), channel_id=2, replica_groups=mesh['groups'=2,'vocab'=16] {'vocab'}, dimensions={0}, use_global_device_ids=true | all-gather | bytes 8704 | tf_op jit(solution)/shard_map/all_gather | solution.py:16
  117.5 3.5 %all-to-all-start.3 = ((s32[16,2,4,128]{3,2,1,0:T(4,128)}), s32[16,2,4,128]{3,2,1,0:T(4,128)S(1)}, u32[]{:S(2)}, u32[]{:S(2)}) async-start(s32[16,2,4,128]{3,2,1,0:T(4,128)} %broadcast_select_fusion.1), calls=%async_computation.3 | async-start | bytes 131072 | tf_op jit(solution)/shard_map/all_to_all | solution.py:104
  121.0 6.8 %all-to-all-done.3 = s32[16,2,4,128]{3,2,1,0:T(4,128)S(1)} async-done(((s32[16,2,4,128]{3,2,1,0:T(4,128)}), s32[16,2,4,128]{3,2,1,0:T(4,128)S(1)}, u32[]{:S(2)}, u32[]{:S(2)}) %all-to-all-start.3) | async-done | bytes 65568 | tf_op jit(solution)/shard_map/all_to_all | solution.py:104
  127.9 3.7 %all-to-all-start.2 = ((bf16[16,2,128,128]{3,2,1,0:T(8,128)(2,1)}), bf16[16,2,128,128]{3,2,1,0:T(8,128)(2,1)S(1)}, u32[]{:S(2)}, u32[]{:S(2)}) async-start(bf16[16,2,128,128]{3,2,1,0:T(8,128)(2,1)} %broadcast_select_fusion), calls=%async_computation.2 | async-start | bytes 2097152 | tf_op jit(solution)/shard_map/all_to_all | solution.py:103
  133.6 20.8 %all-to-all-done.2 = bf16[16,2,128,128]{3,2,1,0:T(8,128)(2,1)S(1)} async-done(((bf16[16,2,128,128]{3,2,1,0:T(8,128)(2,1)}), bf16[16,2,128,128]{3,2,1,0:T(8,128)(2,1)S(1)}, u32[]{:S(2)}, u32[]{:S(2)}) %all-to-all-start.2) | async-done | bytes 1048608 | tf_op jit(solution)/shard_map/all_to_all | solution.py:103
  154.4 1.1 fusion.14
  155.6 1.0 fusion.10
  156.6 1.1 fusion.34
  157.7 34.8 %psum.7 = f32[128]{0:T(128)S(1)} all-reduce(f32[128]{0:T(128)S(1)} %get-tuple-element.119), channel_id=1, replica_groups=mesh['groups'=2,'vocab'=16] {'vocab'}, use_global_device_ids=true, to_apply=%region_12.14 | all-reduce | flops 128 | bytes 1024 | tf_op jit(solution)/shard_map/psum | solution.py:122
  192.5 8.1 %convolution_bitcast_fusion = f32[8192,128]{0,1:T(8,128)} fusion(bf16[8192,512]{1,0:T(8,128)(2,1)} %param.15, f32[512,128]{0,1:T(8,128)S(1)} %get-tuple-element.120, f32[128,512]{1,0:T(8,128)S(1)} %fusion.35, f32[128]{0:T(128)S(1)} %broadcast_add_fusion, f32[128]{0:T(128)S(1)} %copy-done.4), kind=kOutput, calls=%fused_computation.19 | convolution fusion | flops 1074135040 | bytes 13108224 | tf_op jit(solution)/shard_map/dot_general | solution.py:129
  200.7 69.7 %reduce-scatter.2.cloned.1.call-done = f32[512,128]{0,1:T(8,128)} async-done(((f32[8192,128]{0,1:T(8,128)}), f32[512,128]{0,1:T(8,128)}) %reduce-scatter.2.cloned.1.call-update) | async-done | bytes 262160 | tf_op jit(solution)/shard_map/reduce_scatter | solution.py:128
  270.4 1.0 convert_element_type.42
  271.4 0.8 copy.36
  (83 shorter events, 4.9 us)
Async XLA Ops:
  6.5 55.4 %copy-start = (bf16[128,8192]{1,0:T(8,128)(2,1)S(1)}, bf16[128,8192]{1,0:T(8,128)(2,1)}, u32[]{:S(2)}) copy-start(bf16[128,8192]{1,0:T(8,128)(2,1)} %param.14) | copy-start | bytes 6291460
  10.4 82.0 %all-to-all-start.1 = ((s32[16,1,2]{2,1,0:T(1,128)}), s32[16,1,2]{2,1,0:T(1,128)S(1)}, u32[]{:S(2)}, u32[]{:S(2)}) async-start(s32[16,1,2]{2,1,0:T(1,128)} %bitcast.13), calls=%async_computation.1 | async-start | bytes 16384 | tf_op jit(solution)/shard_map/all_to_all | solution.py:106
  61.9 5.0 %copy-start.3 = (s32[32,128]{1,0:T(8,128)S(1)}, s32[32,128]{1,0:T(8,128)}, u32[]{:S(2)}) copy-start(s32[32,128]{1,0:T(8,128)} %param.17) | copy-start | bytes 49156
  62.0 5.6 %copy-start.1 = (bf16[1024,128]{1,0:T(8,128)(2,1)S(1)}, bf16[1024,128]{1,0:T(8,128)(2,1)}, u32[]{:S(2)}) copy-start(bf16[1024,128]{1,0:T(8,128)(2,1)} %param.16) | copy-start | bytes 786436
  66.7 5.8 %copy-start.2 = (s32[24,128]{1,0:T(8,128)S(1)}, s32[24,128]{1,0:T(8,128)}, u32[]{:S(2)}) copy-start(s32[24,128]{1,0:T(8,128)} %param.21) | copy-start | bytes 36868
  92.4 25.1 %all-to-all-start = ((s32[16,2,128]{2,1,0:T(2,128)}), s32[16,2,128]{2,1,0:T(2,128)S(1)}, u32[]{:S(2)}, u32[]{:S(2)}) async-start(s32[16,2,128]{2,1,0:T(2,128)} %select_select_fusion), calls=%async_computation | async-start | bytes 32768 | tf_op jit(solution)/shard_map/all_to_all | solution.py:105
  117.5 10.4 %all-to-all-start.3 = ((s32[16,2,4,128]{3,2,1,0:T(4,128)}), s32[16,2,4,128]{3,2,1,0:T(4,128)S(1)}, u32[]{:S(2)}, u32[]{:S(2)}) async-start(s32[16,2,4,128]{3,2,1,0:T(4,128)} %broadcast_select_fusion.1), calls=%async_computation.3 | async-start | bytes 131072 | tf_op jit(solution)/shard_map/all_to_all | solution.py:104
  127.9 26.6 %all-to-all-start.2 = ((bf16[16,2,128,128]{3,2,1,0:T(8,128)(2,1)}), bf16[16,2,128,128]{3,2,1,0:T(8,128)(2,1)S(1)}, u32[]{:S(2)}, u32[]{:S(2)}) async-start(bf16[16,2,128,128]{3,2,1,0:T(8,128)(2,1)} %broadcast_select_fusion), calls=%async_computation.2 | async-start | bytes 2097152 | tf_op jit(solution)/shard_map/all_to_all | solution.py:103
  131.5 138.9 %reduce-scatter.2.cloned.1.call-start = ((), (), s32[]{:S(2)}) async-start(), calls=%async_computation.5 | async-start | bytes 4456448 | tf_op jit(solution)/shard_map/reduce_scatter | solution.py:128
  133.6 58.8 %copy-start.4 = (f32[128]{0:T(128)S(1)}, f32[128]{0:T(128)}, u32[]{:S(2)}) copy-start(f32[128]{0:T(128)} %log_add_fusion.1) | copy-start | bytes 1540
Sparse Core Ops, SparseCore 0:
  200.8 69.5 reduce-scatter.1
where the time goes:
time: 280 us; the launch traced here: 279 us
  blocking collectives  114 us (41%)
  waiting for transfers between devices  97.4 us (35%)
  starting transfers between devices  18.1 us (6%)
  matrix products  14.9 us (5%)
  between operations  13.7 us (5%)
  other arithmetic  13 us (5%)
  local copies, waits for them, and re-layouts  7.64 us (3%)
    all_gather x4, blocking collectives, merged(): pieces = jax.tree.map(lambda part: lax.all_gather(part, axis), value)  79.1 us
    reduce_scatter x1, waiting for transfers between devices, per_device(): lax.psum_scatter(jnp.dot(student_weight, residual, preferred_element_type...  69.7 us
    psum x1, blocking collectives, per_device(): mass_totals = lax.psum(jnp.sum(mapped, axis=0), 'vocab')  34.8 us
    all_to_all x1, waiting for transfers between devices, per_device(): lax.all_to_all(send_codes, 'vocab', split_axis=0, concat_axis=0, tiled=True)  20.8 us
    dot_general x1, matrix products, per_device(): jnp.dot(student_weight, residual, preferred_element_type=jnp.float32)  8.15 us
    all_to_all x1, starting transfers between devices, per_device(): lax.all_to_all(slot_blocks, 'vocab', split_axis=0, concat_axis=0, tiled=T...  7.39 us
    all_to_all x1, waiting for transfers between devices, per_device(): lax.all_to_all(send_exps, 'vocab', split_axis=0, concat_axis=0, tiled=True)  6.85 us
  transfers between devices with their start and end apart: 5, of which 3 were waited for; matrix products, arithmetic and copies ran while one was open for 7% of the time, Pallas kernels for 0%

commit v1 on v0

v1 whole, which is shorter than its diff:
```python
import functools

import jax
import jax.numpy as jnp
from jax import lax
from jax.experimental import pallas as pl
from jax.experimental.pallas import tpu as pltpu
from jax.sharding import PartitionSpec as P

BLK = 128
CAP = 2
META = 16
GROUP = 32
W_CHUNKS = 8

smoothing = 0.05
loss_scale = 64.0


def grid_of(owners):
    chips = owners // 2
    b = 1
    while (2 * b) * (2 * b) <= chips:
        b *= 2
    return chips // b, b


def kernel(
    n, A, B,
    tile_s, dest_s, block_s, hidden_hbm, w_hbm, codes_ref, exps_ref, map_ref, out_ref,
    w_ref, h_ref, tl_ref, probs_ref, send_ref, recv_ref, stat_send, tstat, sstat, mass, logits_ref, mapped_ref,
    res_ref, p_send, p_own, rc, rb, ra,
    w_sem, h_sem, a2a_send_sem, a2a_recv_sem, small_send_sem, small_recv_sem,
    c_send_sem, c_recv_sem, b_send_sem, b_recv_sem, a_send_sem, a_recv_sem,
):
    me = lax.axis_index("vocab")
    pairs = dest_s.shape[0]
    v_local = w_ref.shape[1]
    d_full = w_ref.shape[0]
    rows = d_full // n
    tokens = h_ref.shape[0]
    tiles = tl_ref.shape[0]
    payload = CAP * BLK
    core = lax.rem(me, 2)
    chip = me // 2
    b_me = lax.rem(chip, B)
    a_me = chip // B

    def at(a, b, c):
        return (a * B + b) * 2 + c

    barrier = pltpu.get_barrier_semaphore()

    def greet(off, carry):
        pl.semaphore_signal(barrier, inc=1, device_id={"vocab": lax.rem(me + off, n)}, device_id_type=pl.DeviceIdType.MESH)
        return carry

    lax.fori_loop(1, n, greet, 0)

    h_copy = pltpu.make_async_copy(hidden_hbm, h_ref, h_sem)
    h_copy.start()
    w_rows = d_full // W_CHUNKS
    w_copies = []
    for c in range(W_CHUNKS):
        part = pl.ds(c * w_rows, w_rows)
        w_copies.append(pltpu.make_async_copy(w_hbm.at[part, :], w_ref.at[part, :], w_sem.at[c]))
        w_copies[-1].start()

    exps = exps_ref[...]
    scales = jnp.where(exps >= 1, 2.0, jnp.where(exps == 0, 1.0, jnp.where(exps == -1, 0.5, 0.25)))
    per_tile = BLK // GROUP
    peak = jnp.full((1, tokens), -jnp.inf, jnp.float32)
    for t in range(tiles):
        codes = codes_ref[t * BLK:(t + 1) * BLK, :].astype(jnp.float32)
        scale = scales[t * per_tile:(t + 1) * per_tile, :]
        values = (codes.reshape(per_tile, GROUP, tokens) * scale[:, None, :]).reshape(BLK, tokens)
        tl_ref[t] = values.astype(jnp.bfloat16)
        peak = jnp.maximum(peak, jnp.max(values, axis=0, keepdims=True))
    total = jnp.zeros((1, tokens), jnp.float32)
    for t in range(tiles):
        total += jnp.sum(jnp.exp(tl_ref[t].astype(jnp.float32) - peak), axis=0, keepdims=True)

    row8 = lax.broadcasted_iota(jnp.int32, (8, tokens), 0)

    def small_copy(which, gathered, off):
        return pltpu.make_async_remote_copy(
            src_ref=stat_send.at[which],
            dst_ref=gathered.at[off],
            send_sem=small_send_sem.at[which],
            recv_sem=small_recv_sem.at[which],
            device_id={"vocab": lax.rem(me + off, n)},
            device_id_type=pl.DeviceIdType.MESH,
        )

    def share(which, gathered, tile):
        stat_send[which] = tile
        gathered[0] = tile

        def one(off, carry):
            small_copy(which, gathered, off).start()
            return carry

        lax.fori_loop(1, n, one, 0)

    def collect(which, gathered):
        others = gathered.at[pl.ds(1, n - 1)]
        pltpu.make_async_copy(others, others, small_recv_sem.at[which]).wait()

    def normalizer(gathered):
        peaks = gathered[:, 0, :]
        totals = gathered[:, 1, :]
        top = jnp.max(peaks, axis=0, keepdims=True)
        return top + jnp.log(jnp.sum(totals * jnp.exp(peaks - top), axis=0, keepdims=True))

    pl.semaphore_wait(barrier, n - 1)
    share(0, tstat, jnp.where(row8 == 0, peak, total))

    meta_row = lax.broadcasted_iota(jnp.int32, (META, BLK), 0)

    def fill(off, ref):
        target = lax.rem(me + off, n)

        def look(k, found):
            first, second = found
            hit = dest_s[k] == target
            second = jnp.where(hit & (first >= 0), k, second)
            first = jnp.where(hit & (first < 0), k, first)
            return first, second

        first, second = lax.fori_loop(0, pairs, look, (jnp.int32(-1), jnp.int32(-1)), unroll=8)
        meta = jnp.zeros((META, BLK), jnp.float32)
        for slot, source in enumerate((first, second)):
            index = jnp.maximum(source, 0)
            ref[off, slot * BLK:(slot + 1) * BLK, :] = tl_ref[tile_s[index]]
            entries = jnp.minimum(map_ref[pl.ds(index, 1), :], BLK)
            entries = jnp.where(source >= 0, entries, BLK).astype(jnp.float32)
            block = block_s[index].astype(jnp.float32)
            meta = jnp.where(meta_row == slot, entries, meta)
            meta = jnp.where(meta_row == CAP + slot, block, meta)
        ref[off, payload:payload + META, :] = meta.astype(jnp.bfloat16)

    def slot_copy(off):
        return pltpu.make_async_remote_copy(
            src_ref=send_ref.at[off],
            dst_ref=recv_ref.at[off],
            send_sem=a2a_send_sem,
            recv_sem=a2a_recv_sem.at[off],
            device_id={"vocab": lax.rem(me + off, n)},
            device_id_type=pl.DeviceIdType.MESH,
        )

    def send_slot(off, carry):
        fill(off, send_ref)
        slot_copy(off).start()
        return carry

    lax.fori_loop(1, n, send_slot, 0)
    fill(0, recv_ref)

    h_copy.wait()
    logits = jnp.zeros((tokens, v_local), jnp.float32)
    for c in range(W_CHUNKS):
        w_copies[c].wait()
        logits += jnp.dot(
            h_ref[:, c * w_rows:(c + 1) * w_rows],
            w_ref[c * w_rows:(c + 1) * w_rows, :],
            preferred_element_type=jnp.float32,
        )
    logits = logits.T
    logits_ref[...] = logits
    s_peak = jnp.max(logits, axis=0, keepdims=True)
    s_total = jnp.sum(jnp.exp(logits - s_peak), axis=0, keepdims=True)
    share(1, sstat, jnp.where(row8 == 0, s_peak, s_total))

    collect(0, tstat)
    lse = normalizer(tstat)
    tile_row = lax.broadcasted_iota(jnp.int32, (tiles, BLK), 0)

    def count(k, counts):
        valid = jnp.where(map_ref[pl.ds(k, 1), :] < BLK, 1.0, 0.0)
        return counts + jnp.where(tile_row == tile_s[k], valid, 0.0)

    counts = lax.fori_loop(0, pairs, count, jnp.zeros((tiles, BLK), jnp.float32))
    counts = counts.astype(jnp.bfloat16)
    part_mass = jnp.zeros((tiles, tokens), jnp.float32)
    for t in range(tiles):
        probs = jnp.exp(tl_ref[t].astype(jnp.float32) - lse).astype(jnp.bfloat16)
        term = jnp.dot(counts, probs, preferred_element_type=jnp.float32)
        part_mass += jnp.where(lax.broadcasted_iota(jnp.int32, (tiles, tokens), 0) == t, term, 0.0)
    part_mass = jnp.sum(part_mass, axis=0, keepdims=True)
    share(2, mass, jnp.broadcast_to(part_mass, (8, tokens)))

    mapped_ref[...] = jnp.zeros_like(mapped_ref)
    entry = lax.broadcasted_iota(jnp.int32, (v_local, BLK), 0).astype(jnp.float32)

    def join(off):
        probs_ref[...] = jnp.exp(recv_ref[off, 0:payload, :].astype(jnp.float32) - lse).astype(jnp.bfloat16)
        meta = recv_ref[off, payload:payload + META, :].astype(jnp.float32)
        pickers = []
        for slot in range(CAP):
            entries = meta[slot:slot + 1, :]
            blocks = meta[CAP + slot:CAP + slot + 1, :]
            places = jnp.where(entries < BLK, blocks * BLK + entries, float(v_local))
            pickers.append(jnp.where(entry == places, 1.0, 0.0).astype(jnp.bfloat16))
        picker = jnp.concatenate(pickers, axis=1)
        mapped_ref[...] += jnp.dot(picker, probs_ref[...], preferred_element_type=jnp.float32)

    join(0)

    def join_next(off, carry):
        slot_copy(off).wait_recv()
        join(off)
        return carry

    lax.fori_loop(1, n, join_next, 0)

    collect(1, sstat)
    collect(2, mass)
    s_lse = normalizer(sstat)
    mass_total = jnp.sum(mass[:, 0, :], axis=0, keepdims=True)
    target = (mapped_ref[...] + smoothing / (v_local * n)) / (mass_total + smoothing)
    s_probs = jnp.exp(logits_ref[...] - s_lse)
    res_ref[...] = (loss_scale * (s_probs - target)).astype(jnp.bfloat16)

    def core_copy(i, j):
        idx = i * B + j
        return pltpu.make_async_remote_copy(
            src_ref=p_send.at[idx], dst_ref=rc.at[idx],
            send_sem=c_send_sem, recv_sem=c_recv_sem.at[idx],
            device_id={"vocab": at(a_me, b_me, 1 - core)}, device_id_type=pl.DeviceIdType.MESH,
        )

    def b_copy(i, j):
        return pltpu.make_async_remote_copy(
            src_ref=p_own.at[i * B + j], dst_ref=rb.at[i * (B - 1) + j],
            send_sem=b_send_sem, recv_sem=b_recv_sem.at[i * (B - 1) + j],
            device_id={"vocab": at(a_me, lax.rem(b_me + 1 + j, B), core)}, device_id_type=pl.DeviceIdType.MESH,
        )

    def a_copy(i):
        return pltpu.make_async_remote_copy(
            src_ref=p_own.at[i * B + B - 1], dst_ref=ra.at[i],
            send_sem=a_send_sem, recv_sem=a_recv_sem.at[i],
            device_id={"vocab": at(lax.rem(a_me + 1 + i, A), b_me, core)}, device_id_type=pl.DeviceIdType.MESH,
        )

    def product(i, j, c):
        owner = at(lax.rem(a_me + 1 + i, A), lax.rem(b_me + 1 + j, B), c)
        start = pl.multiple_of(owner * rows, rows)
        return jnp.dot(w_ref[pl.ds(start, rows), :], res_ref[...], preferred_element_type=jnp.float32)

    for i in range(A + 2):
        if i < A:
            def produce(j, carry, i=i):
                p_send[i * B + j] = product(i, j, 1 - core)
                core_copy(i, j).start()
                p_own[i * B + j] = product(i, j, core)
                return carry

            lax.fori_loop(0, B, produce, 0)
        if 1 <= i <= A:
            q = i - 1
            for j in range(B):
                core_copy(q, j).wait_recv()
                p_own[q * B + j] += rc[q * B + j]
                if j < B - 1:
                    b_copy(q, j).start()
        if i >= 2:
            q = i - 2
            acc = p_own[q * B + B - 1]
            for j in range(B - 1):
                b_copy(q, j).wait_recv()
                acc += rb[q * (B - 1) + j]
            p_own[q * B + B - 1] = acc
            if q < A - 1:
                a_copy(q).start()

    acc = p_own[A * B - 1]
    for i in range(A - 1):
        a_copy(i).wait_recv()
        acc += ra[i]
    out_ref[...] = acc.astype(jnp.bfloat16)

    def drained(ref, sem):
        pltpu.make_async_copy(ref, ref, sem).wait()

    drained(send_ref.at[pl.ds(1, n - 1)], a2a_send_sem)
    for which, gathered in enumerate((tstat, sstat, mass)):
        drained(gathered.at[pl.ds(1, n - 1)], small_send_sem.at[which])
    drained(p_send, c_send_sem)
    drained(rb, b_send_sem)
    drained(ra, a_send_sem)


def per_device(
    n, hidden, student_weight, teacher_codes, teacher_exps, pair_tile, pair_dest, pair_block, pair_map
):
    A, B = grid_of(n)
    tokens, d_full = hidden.shape
    v_local = student_weight.shape[1]
    rows = d_full // n
    tiles = teacher_codes.shape[0] // BLK
    slot_rows = CAP * BLK + META
    f32, bf16 = jnp.float32, jnp.bfloat16
    vmem = pl.BlockSpec(memory_space=pltpu.VMEM)
    smem = pl.BlockSpec(memory_space=pltpu.SMEM)
    hbm = pl.BlockSpec(memory_space=pl.ANY)
    dma = pltpu.SemaphoreType.DMA
    return pl.pallas_call(
        functools.partial(kernel, n, A, B),
        out_shape=jax.ShapeDtypeStruct((rows, tokens), bf16),
        in_specs=[smem, smem, smem, hbm, hbm, vmem, vmem, vmem],
        out_specs=vmem,
        scratch_shapes=[
            pltpu.VMEM((d_full, v_local), bf16),
            pltpu.VMEM((tokens, d_full), bf16),
            pltpu.VMEM((tiles, BLK, tokens), bf16),
            pltpu.VMEM((CAP * BLK, tokens), bf16),
            pltpu.VMEM((n, slot_rows, tokens), bf16),
            pltpu.VMEM((n, slot_rows, tokens), bf16),
            pltpu.VMEM((3, 8, tokens), f32),
            pltpu.VMEM((n, 8, tokens), f32),
            pltpu.VMEM((n, 8, tokens), f32),
            pltpu.VMEM((n, 8, tokens), f32),
            pltpu.VMEM((v_local, tokens), f32),
            pltpu.VMEM((v_local, tokens), f32),
            pltpu.VMEM((v_local, tokens), bf16),
            pltpu.VMEM((A * B, rows, tokens), f32),
            pltpu.VMEM((A * B, rows, tokens), f32),
            pltpu.VMEM((A * B, rows, tokens), f32),
            pltpu.VMEM((A * (B - 1), rows, tokens), f32),
            pltpu.VMEM((A - 1, rows, tokens), f32),
            dma((W_CHUNKS,)),
            dma,
            dma,
            dma((n,)),
            dma((3,)),
            dma((3,)),
            dma,
            dma((A * B,)),
            dma,
            dma((A * (B - 1),)),
            dma,
            dma((A - 1,)),
        ],
        compiler_params=pltpu.CompilerParams(
            collective_id=0, has_side_effects=True, vmem_limit_bytes=56 * 1024 * 1024
        ),
    )(
        pair_tile, pair_dest.reshape(-1), pair_block,
        hidden, student_weight, teacher_codes, teacher_exps, pair_map,
    )


def solution(mesh):
    return jax.shard_map(
        functools.partial(per_device, mesh.shape["vocab"]),
        mesh=mesh,
        in_specs=(
            P("groups", None),
            P(None, "vocab"),
            P("vocab", "groups"),
            P("vocab", "groups"),
            P("vocab"),
            P("vocab", None),
            P("vocab"),
            P("vocab", None),
        ),
        out_specs=P("vocab", "groups"),
        check_vma=False,
    )
```

time: 280 us -> 74.6 us (0.27)
  blocking collectives: 114 us -> 0 us
  waiting for transfers between devices: 97.4 us -> 0 us
  Pallas kernels: 0 us -> 72.9 us
  starting transfers between devices: 18.1 us -> 0 us
  matrix products: 14.9 us -> 0 us
  between operations: 13.7 us -> 0.01 us
  other arithmetic: 13 us -> 0 us
  local copies, waits for them, and re-layouts: 7.64 us -> 1.57 us
    all_gather x4 -> x0, blocking collectives: 79.1 us -> none  [merged(): pieces = jax.tree.map(lambda part: lax.all_gather(part, axis), value)]
    pallas_call x0 -> x1, Pallas kernels: none -> 72.9 us  [per_device(): pl.pallas_call(functools.partial(kernel, n, A, B), out_shape=jax.ShapeDty...]
    reduce_scatter x1 -> x0, waiting for transfers between devices: 69.7 us -> none  [per_device(): lax.psum_scatter(jnp.dot(student_weight, residual, preferred_element_type...]
    psum x1 -> x0, blocking collectives: 34.8 us -> none  [per_device(): mass_totals = lax.psum(jnp.sum(mapped, axis=0), 'vocab')]
    all_to_all x4 -> x0, waiting for transfers between devices: 27.6 us -> none  [the longest x1 20.8 us: per_device(): lax.all_to_all(send_codes, 'vocab', split_axis=0, concat_axis=0, tiled=True)]
    all_to_all x4 -> x0, starting transfers between devices: 18 us -> none  [the longest x1 7.39 us: per_device(): lax.all_to_all(slot_blocks, 'vocab', split_axis=0, concat_axis=0, tiled=T...]
    dot_general x4 -> x0, matrix products: 14.9 us -> none  [the longest x1 8.15 us: per_device(): jnp.dot(student_weight, residual, preferred_element_type=jnp.float32)]
    gather x5 -> x0, local copies, waits for them, and re-layouts: 5.6 us -> none  [the longest x1 1.72 us: per_device(): jnp.take(teacher_codes.reshape(-1, BLK, tokens), slot_tiles, axis=0)]
  transfers between devices with their start and end apart: 5 -> 0, of which waited for: 3 -> 0; matrix products, arithmetic and copies ran while one was open for 7% -> 0% of each run, Pallas kernels for 0% -> 0%
where the time goes in v1:
time: 74.6 us; the launch traced here: 74.5 us
  Pallas kernels  72.9 us (98%)
  local copies, waits for them, and re-layouts  1.57 us (2%)
    pallas_call x1, Pallas kernels, per_device(): pl.pallas_call(functools.partial(kernel, n, A, B), out_shape=jax.ShapeDty...  72.9 us
    unnamed x1, local copies, waits for them, and re-layouts  1.57 us

profile of v1, /device:TPU:0, one launch (start us, length us, event | category | flops | bytes accessed | tf_op | source)
XLA Modules:
  0.0 74.5 jit_solution(4753806447592929212)
XLA Ops:
  0.0 72.9 %shard_map.82 = bf16[512,128]{1,0:T(8,128)(2,1)} custom-call(s32[24]{0:T(128)} %tile_s.1, s32[24]{0:T(128)} %bitcast.1, s32[24]{0:T(128)} %block_s.1, bf16[128,8192]{1,0:T(8,128)(2,1)} %hidden_hbm.1, bf16[8192,512]{1,0:T(8,128)(2,1)} %w_hbm.1, bf16[1024,128]{1,0:T(8,128)(2,1)} %codes_ref.1, s32[32,128]{1,0:T(8,128)} %exps_ref.1, s32[24,128]{1,0:T(8,128)} %map_ref.1), custom_call_target="tpu_custom_call" | custom-call | tf_op jit(solution)/shard_map/pallas_call | solution.py:309
  72.9 1.6 %copy.10 = bf16[512,128]{1,0:T(8,128)(2,1)} copy(bf16[512,128]{1,0:T(8,128)(2,1)} %shard_map.82) | data formatting | bytes 262144

commit v2 on v1

--- a/solution.py
+++ b/solution.py
@@ -12,6 +12,9 @@
 META = 16
 GROUP = 32
 W_CHUNKS = 8
+SCALE_ROWS = 16
+TOP_CODE = 32000.0
+TINY = 1e-30
 
 smoothing = 0.05
 loss_scale = 64.0
@@ -25,11 +28,29 @@
     return chips // b, b
 
 
+def encode(values, ref):
+    rows = values.shape[0]
+    top = jnp.maximum(jnp.max(jnp.abs(values), axis=0, keepdims=True), TINY)
+    level = jnp.ceil(8.0 * jnp.log2(top))
+    step = TOP_CODE / jnp.exp2(level * 0.125)
+    codes = jnp.round(values * step).astype(jnp.int32)
+    ref[0:rows, :] = codes.astype(jnp.int16)
+    levels = jnp.broadcast_to(level, (SCALE_ROWS, values.shape[1])).astype(jnp.int32)
+    ref[rows:rows + SCALE_ROWS, :] = levels.astype(jnp.int16)
+
+
+def decode(ref):
+    rows = ref.shape[0] - SCALE_ROWS
+    level = ref[rows:rows + SCALE_ROWS, :].astype(jnp.int32).astype(jnp.float32)[0:1, :]
+    scale = jnp.exp2(level * 0.125) * (1.0 / TOP_CODE)
+    return ref[0:rows, :].astype(jnp.int32).astype(jnp.float32) * scale
+
+
 def kernel(
     n, A, B,
     tile_s, dest_s, block_s, hidden_hbm, w_hbm, codes_ref, exps_ref, map_ref, out_ref,
     w_ref, h_ref, tl_ref, probs_ref, send_ref, recv_ref, stat_send, tstat, sstat, mass, logits_ref, mapped_ref,
-    res_ref, p_send, p_own, rc, rb, ra,
+    res_ref, p_send, p_own, rc, sb, sa, rb, ra,
     w_sem, h_sem, a2a_send_sem, a2a_recv_sem, small_send_sem, small_recv_sem,
     c_send_sem, c_recv_sem, b_send_sem, b_recv_sem, a_send_sem, a_recv_sem,
 ):
@@ -149,12 +170,17 @@
             device_id_type=pl.DeviceIdType.MESH,
         )
 
-    def send_slot(off, carry):
+    def far_first(i):
+        odd = lax.rem(i, 2)
+        return n // 2 + odd * ((i + 1) // 2) - (1 - odd) * (i // 2)
+
+    def send_slot(i, carry):
+        off = far_first(i)
         fill(off, send_ref)
         slot_copy(off).start()
         return carry
 
-    lax.fori_loop(1, n, send_slot, 0)
+    lax.fori_loop(0, n - 1, send_slot, 0)
     fill(0, recv_ref)
 
     h_copy.wait()
@@ -207,12 +233,13 @@
 
     join(0)
 
-    def join_next(off, carry):
+    def join_next(i, carry):
+        off = far_first(i)
         slot_copy(off).wait_recv()
         join(off)
         return carry
 
-    lax.fori_loop(1, n, join_next, 0)
+    lax.fori_loop(0, n - 1, join_next, 0)
 
     collect(1, sstat)
     collect(2, mass)
@@ -232,14 +259,14 @@
 
     def b_copy(i, j):
         return pltpu.make_async_remote_copy(
-            src_ref=p_own.at[i * B + j], dst_ref=rb.at[i * (B - 1) + j],
+            src_ref=sb.at[i * (B - 1) + j], dst_ref=rb.at[i * (B - 1) + j],
             send_sem=b_send_sem, recv_sem=b_recv_sem.at[i * (B - 1) + j],
             device_id={"vocab": at(a_me, lax.rem(b_me + 1 + j, B), core)}, device_id_type=pl.DeviceIdType.MESH,
         )
 
     def a_copy(i):
         return pltpu.make_async_remote_copy(
-            src_ref=p_own.at[i * B + B - 1], dst_ref=ra.at[i],
+            src_ref=sa.at[i], dst_ref=ra.at[i],
             send_sem=a_send_sem, recv_sem=a_recv_sem.at[i],
             device_id={"vocab": at(lax.rem(a_me + 1 + i, A), b_me, core)}, device_id_type=pl.DeviceIdType.MESH,
         )
@@ -262,23 +289,25 @@
             q = i - 1
             for j in range(B):
                 core_copy(q, j).wait_recv()
-                p_own[q * B + j] += rc[q * B + j]
+                both = p_own[q * B + j] + rc[q * B + j]
                 if j < B - 1:
+                    encode(both, sb.at[q * (B - 1) + j])
                     b_copy(q, j).start()
+                else:
+                    p_own[q * B + j] = both
         if i >= 2:
             q = i - 2
             acc = p_own[q * B + B - 1]
             for j in range(B - 1):
                 b_copy(q, j).wait_recv()
-                acc += rb[q * (B - 1) + j]
-            p_own[q * B + B - 1] = acc
+                acc += decode(rb.at[q * (B - 1) + j])
             if q < A - 1:
+                encode(acc, sa.at[q])
                 a_copy(q).start()
 
-    acc = p_own[A * B - 1]
     for i in range(A - 1):
         a_copy(i).wait_recv()
-        acc += ra[i]
+        acc += decode(ra.at[i])
     out_ref[...] = acc.astype(jnp.bfloat16)
 
     def drained(ref, sem):
@@ -328,8 +357,10 @@
             pltpu.VMEM((A * B, rows, tokens), f32),
             pltpu.VMEM((A * B, rows, tokens), f32),
             pltpu.VMEM((A * B, rows, tokens), f32),
-            pltpu.VMEM((A * (B - 1), rows, tokens), f32),
-            pltpu.VMEM((A - 1, rows, tokens), f32),
+            pltpu.VMEM((A * (B - 1), rows + SCALE_ROWS, tokens), jnp.int16),
+            pltpu.VMEM((A - 1, rows + SCALE_ROWS, tokens), jnp.int16),
+            pltpu.VMEM((A * (B - 1), rows + SCALE_ROWS, tokens), jnp.int16),
+            pltpu.VMEM((A - 1, rows + SCALE_ROWS, tokens), jnp.int16),
             dma((W_CHUNKS,)),
             dma,
             dma,

time: 74.6 us -> 61.5 us (0.82)
  Pallas kernels: 72.9 us -> 59.8 us
    pallas_call x1, Pallas kernels: 72.9 us -> 59.8 us  [per_device(): pl.pallas_call(functools.partial(kernel, n, A, B), out_shape=jax.ShapeDty...]
where the time goes in v2:
time: 61.5 us; the launch traced here: 61.3 us
  Pallas kernels  59.8 us (97%)
  local copies, waits for them, and re-layouts  1.57 us (3%)
    pallas_call x1, Pallas kernels, per_device(): pl.pallas_call(functools.partial(kernel, n, A, B), out_shape=jax.ShapeDty...  59.8 us
    unnamed x1, local copies, waits for them, and re-layouts  1.57 us

profile of v2, /device:TPU:0, one launch (start us, length us, event | category | flops | bytes accessed | tf_op | source)
XLA Modules:
  0.0 61.3 jit_solution(6665705766829692092)
XLA Ops:
  0.0 59.8 %shard_map.82 = bf16[512,128]{1,0:T(8,128)(2,1)} custom-call(s32[24]{0:T(128)} %tile_s.1, s32[24]{0:T(128)} %bitcast.1, s32[24]{0:T(128)} %block_s.1, bf16[128,8192]{1,0:T(8,128)(2,1)} %hidden_hbm.1, bf16[8192,512]{1,0:T(8,128)(2,1)} %w_hbm.1, bf16[1024,128]{1,0:T(8,128)(2,1)} %codes_ref.1, s32[32,128]{1,0:T(8,128)} %exps_ref.1, s32[24,128]{1,0:T(8,128)} %map_ref.1), custom_call_target="tpu_custom_call" | custom-call | tf_op jit(solution)/shard_map/pallas_call | solution.py:338
  59.8 1.6 %copy.10 = bf16[512,128]{1,0:T(8,128)(2,1)} copy(bf16[512,128]{1,0:T(8,128)(2,1)} %shard_map.82) | data formatting | bytes 262144

commit v3 on v2

--- a/solution.py
+++ b/solution.py
@@ -13,6 +13,7 @@
 GROUP = 32
 W_CHUNKS = 8
 SCALE_ROWS = 16
+CUTS = 1
 TOP_CODE = 32000.0
 TINY = 1e-30
 
@@ -170,18 +171,22 @@
             device_id_type=pl.DeviceIdType.MESH,
         )
 
-    def far_first(i):
+    def spread(i, size):
         odd = lax.rem(i, 2)
-        return n // 2 + odd * ((i + 1) // 2) - (1 - odd) * (i // 2)
+        return size // 2 + odd * ((i + 1) // 2) - (1 - odd) * (i // 2)
+
+    def slot_order(i):
+        odd = lax.rem(i, 2)
+        return spread(odd * (n - 2 - i // 2) + (1 - odd) * (i // 2), n)
 
     def send_slot(i, carry):
-        off = far_first(i)
+        off = slot_order(i)
         fill(off, send_ref)
         slot_copy(off).start()
         return carry
 
-    lax.fori_loop(0, n - 1, send_slot, 0)
-    fill(0, recv_ref)
+    early = n // 3
+    lax.fori_loop(0, early, send_slot, 0)
 
     h_copy.wait()
     logits = jnp.zeros((tokens, v_local), jnp.float32)
@@ -215,6 +220,9 @@
         part_mass += jnp.where(lax.broadcasted_iota(jnp.int32, (tiles, tokens), 0) == t, term, 0.0)
     part_mass = jnp.sum(part_mass, axis=0, keepdims=True)
     share(2, mass, jnp.broadcast_to(part_mass, (8, tokens)))
+
+    lax.fori_loop(early, n - 1, send_slot, 0)
+    fill(0, recv_ref)
 
     mapped_ref[...] = jnp.zeros_like(mapped_ref)
     entry = lax.broadcasted_iota(jnp.int32, (v_local, BLK), 0).astype(jnp.float32)
@@ -234,7 +242,7 @@
     join(0)
 
     def join_next(i, carry):
-        off = far_first(i)
+        off = slot_order(i)
         slot_copy(off).wait_recv()
         join(off)
         return carry
@@ -249,6 +257,12 @@
     s_probs = jnp.exp(logits_ref[...] - s_lse)
     res_ref[...] = (loss_scale * (s_probs - target)).astype(jnp.bfloat16)
 
+    cut = rows // CUTS
+    steps = A * CUTS
+
+    def a_of(i):
+        return lax.rem(a_me + spread(i // CUTS, A), A)
+
     def core_copy(i, j):
         idx = i * B + j
         return pltpu.make_async_remote_copy(
@@ -268,47 +282,46 @@
         return pltpu.make_async_remote_copy(
             src_ref=sa.at[i], dst_ref=ra.at[i],
             send_sem=a_send_sem, recv_sem=a_recv_sem.at[i],
-            device_id={"vocab": at(lax.rem(a_me + 1 + i, A), b_me, core)}, device_id_type=pl.DeviceIdType.MESH,
+            device_id={"vocab": at(a_of(i), b_me, core)}, device_id_type=pl.DeviceIdType.MESH,
         )
 
     def product(i, j, c):
-        owner = at(lax.rem(a_me + 1 + i, A), lax.rem(b_me + 1 + j, B), c)
-        start = pl.multiple_of(owner * rows, rows)
-        return jnp.dot(w_ref[pl.ds(start, rows), :], res_ref[...], preferred_element_type=jnp.float32)
-
-    for i in range(A + 2):
-        if i < A:
-            def produce(j, carry, i=i):
-                p_send[i * B + j] = product(i, j, 1 - core)
-                core_copy(i, j).start()
-                p_own[i * B + j] = product(i, j, core)
-                return carry
-
-            lax.fori_loop(0, B, produce, 0)
-        if 1 <= i <= A:
-            q = i - 1
-            for j in range(B):
-                core_copy(q, j).wait_recv()
-                both = p_own[q * B + j] + rc[q * B + j]
-                if j < B - 1:
-                    encode(both, sb.at[q * (B - 1) + j])
-                    b_copy(q, j).start()
-                else:
-                    p_own[q * B + j] = both
-        if i >= 2:
-            q = i - 2
-            acc = p_own[q * B + B - 1]
-            for j in range(B - 1):
-                b_copy(q, j).wait_recv()
-                acc += decode(rb.at[q * (B - 1) + j])
-            if q < A - 1:
-                encode(acc, sa.at[q])
-                a_copy(q).start()
-
-    for i in range(A - 1):
+        owner = at(a_of(i), lax.rem(b_me + 1 + j, B), c)
+        start = pl.multiple_of(owner * rows + lax.rem(i, CUTS) * cut, cut)
+        return jnp.dot(w_ref[pl.ds(start, cut), :], res_ref[...], preferred_element_type=jnp.float32)
+
+    def step(i, carry):
+        for j in range(B):
+            p_send[i * B + j] = product(i, j, 1 - core)
+            core_copy(i, j).start()
+            if j >= 1:
+                pass_on(i, j - 1)
+            p_own[i * B + j] = product(i, j, core)
+        return carry
+
+    def pass_on(i, j):
+        core_copy(i, j).wait_recv()
+        encode(p_own[i * B + j] + rc[i * B + j], sb.at[i * (B - 1) + j])
+        b_copy(i, j).start()
+
+    def collected(i):
+        core_copy(i, B - 1).wait_recv()
+        acc = p_own[i * B + B - 1] + rc[i * B + B - 1]
+        for j in range(B - 1):
+            b_copy(i, j).wait_recv()
+            acc += decode(rb.at[i * (B - 1) + j])
+        return acc
+
+    lax.fori_loop(0, steps, step, 0)
+    for i in range(steps - CUTS):
+        encode(collected(i), sa.at[i])
+        a_copy(i).start()
+    for s in range(CUTS):
+        out_ref[s * cut:(s + 1) * cut, :] = collected(steps - CUTS + s)
+    for i in range(steps - CUTS):
+        part = (i % CUTS) * cut
         a_copy(i).wait_recv()
-        acc += decode(ra.at[i])
-    out_ref[...] = acc.astype(jnp.bfloat16)
+        out_ref[part:part + cut, :] += decode(ra.at[i])
 
     def drained(ref, sem):
         pltpu.make_async_copy(ref, ref, sem).wait()
@@ -328,6 +341,7 @@
     tokens, d_full = hidden.shape
     v_local = student_weight.shape[1]
     rows = d_full // n
+    cut = rows // CUTS
     tiles = teacher_codes.shape[0] // BLK
     slot_rows = CAP * BLK + META
     f32, bf16 = jnp.float32, jnp.bfloat16
@@ -337,7 +351,7 @@
     dma = pltpu.SemaphoreType.DMA
     return pl.pallas_call(
         functools.partial(kernel, n, A, B),
-        out_shape=jax.ShapeDtypeStruct((rows, tokens), bf16),
+        out_shape=jax.ShapeDtypeStruct((rows, tokens), f32),
         in_specs=[smem, smem, smem, hbm, hbm, vmem, vmem, vmem],
         out_specs=vmem,
         scratch_shapes=[
@@ -354,13 +368,13 @@
             pltpu.VMEM((v_local, tokens), f32),
             pltpu.VMEM((v_local, tokens), f32),
             pltpu.VMEM((v_local, tokens), bf16),
-            pltpu.VMEM((A * B, rows, tokens), f32),
-            pltpu.VMEM((A * B, rows, tokens), f32),
-            pltpu.VMEM((A * B, rows, tokens), f32),
-            pltpu.VMEM((A * (B - 1), rows + SCALE_ROWS, tokens), jnp.int16),
-            pltpu.VMEM((A - 1, rows + SCALE_ROWS, tokens), jnp.int16),
-            pltpu.VMEM((A * (B - 1), rows + SCALE_ROWS, tokens), jnp.int16),
-            pltpu.VMEM((A - 1, rows + SCALE_ROWS, tokens), jnp.int16),
+            pltpu.VMEM((A * CUTS * B, cut, tokens), f32),
+            pltpu.VMEM((A * CUTS * B, cut, tokens), f32),
+            pltpu.VMEM((A * CUTS * B, cut, tokens), f32),
+            pltpu.VMEM((A * CUTS * (B - 1), cut + SCALE_ROWS, tokens), jnp.int16),
+            pltpu.VMEM(((A - 1) * CUTS, cut + SCALE_ROWS, tokens), jnp.int16),
+            pltpu.VMEM((A * CUTS * (B - 1), cut + SCALE_ROWS, tokens), jnp.int16),
+            pltpu.VMEM(((A - 1) * CUTS, cut + SCALE_ROWS, tokens), jnp.int16),
             dma((W_CHUNKS,)),
             dma,
             dma,
@@ -368,11 +382,11 @@
             dma((3,)),
             dma((3,)),
             dma,
-            dma((A * B,)),
+            dma((A * CUTS * B,)),
             dma,
-            dma((A * (B - 1),)),
+            dma((A * CUTS * (B - 1),)),
             dma,
-            dma((A - 1,)),
+            dma(((A - 1) * CUTS,)),
         ],
         compiler_params=pltpu.CompilerParams(
             collective_id=0, has_side_effects=True, vmem_limit_bytes=56 * 1024 * 1024
@@ -380,7 +394,7 @@
     )(
         pair_tile, pair_dest.reshape(-1), pair_block,
         hidden, student_weight, teacher_codes, teacher_exps, pair_map,
-    )
+    ).astype(bf16)
 
 
 def solution(mesh):

time: 61.5 us -> 59.7 us (0.971)
  Pallas kernels: 59.8 us -> 57.9 us
  other arithmetic: 0 us -> 1.62 us
  local copies, waits for them, and re-layouts: 1.57 us -> 0 us
    pallas_call x1, Pallas kernels: 59.8 us -> 57.9 us  [per_device(): pl.pallas_call(functools.partial(kernel, n, A, B), out_shape=jax.ShapeDty...]
    convert_element_type x0 -> x1, other arithmetic: none -> 1.62 us  [per_device(): return pl.pallas_call(functools.partial(kernel, n, A, B), out_shape=jax.S...]
    unnamed x1 -> x0, local copies, waits for them, and re-layouts: 1.57 us -> none
where the time goes in v3:
time: 59.7 us; the launch traced here: 59.6 us
  Pallas kernels  57.9 us (97%)
  other arithmetic  1.62 us (3%)
    pallas_call x1, Pallas kernels, per_device(): pl.pallas_call(functools.partial(kernel, n, A, B), out_shape=jax.ShapeDty...  57.9 us
    convert_element_type x1, other arithmetic, per_device(): return pl.pallas_call(functools.partial(kernel, n, A, B), out_shape=jax.S...  1.62 us

profile of v3, /device:TPU:0, one launch (start us, length us, event | category | flops | bytes accessed | tf_op | source)
XLA Modules:
  0.0 59.6 jit_solution(10375702476844408093)
XLA Ops:
  0.0 57.9 %shard_map.82 = f32[512,128]{1,0:T(8,128)} custom-call(s32[24]{0:T(128)} %tile_s.1, s32[24]{0:T(128)} %bitcast.1, s32[24]{0:T(128)} %block_s.1, bf16[128,8192]{1,0:T(8,128)(2,1)} %hidden_hbm.1, bf16[8192,512]{1,0:T(8,128)(2,1)} %w_hbm.1, bf16[1024,128]{1,0:T(8,128)(2,1)} %codes_ref.1, s32[32,128]{1,0:T(8,128)} %exps_ref.1, s32[24,128]{1,0:T(8,128)} %map_ref.1), custom_call_target="tpu_custom_call" | custom-call | tf_op jit(solution)/shard_map/pallas_call | solution.py:352
  58.0 1.6 %convert_element_type.3 = bf16[512,128]{1,0:T(8,128)(2,1)} convert(f32[512,128]{1,0:T(8,128)} %shard_map.82) | non-fusion elementwise | flops 65536 | bytes 393216 | tf_op jit(solution)/shard_map/convert_element_type | solution.py:397

commit v4 on v3

--- a/solution.py
+++ b/solution.py
@@ -9,7 +9,6 @@
 
 BLK = 128
 CAP = 2
-META = 16
 GROUP = 32
 W_CHUNKS = 8
 SCALE_ROWS = 16
@@ -50,9 +49,9 @@
 def kernel(
     n, A, B,
     tile_s, dest_s, block_s, hidden_hbm, w_hbm, codes_ref, exps_ref, map_ref, out_ref,
-    w_ref, h_ref, tl_ref, probs_ref, send_ref, recv_ref, stat_send, tstat, sstat, mass, logits_ref, mapped_ref,
+    w_ref, h_ref, tl_ref, probs_ref, send_ref, recv_ref, send_meta, recv_meta, stat_send, tstat, sstat, mass, logits_ref, mapped_ref,
     res_ref, p_send, p_own, rc, sb, sa, rb, ra,
-    w_sem, h_sem, a2a_send_sem, a2a_recv_sem, small_send_sem, small_recv_sem,
+    w_sem, h_sem, a2a_send_sem, a2a_recv_sem, meta_send_sem, meta_recv_sem, small_send_sem, small_recv_sem,
     c_send_sem, c_recv_sem, b_send_sem, b_recv_sem, a_send_sem, a_recv_sem,
 ):
     me = lax.axis_index("vocab")
@@ -137,9 +136,8 @@
     pl.semaphore_wait(barrier, n - 1)
     share(0, tstat, jnp.where(row8 == 0, peak, total))
 
-    meta_row = lax.broadcasted_iota(jnp.int32, (META, BLK), 0)
-
-    def fill(off, ref):
+
+    def fill(off, ref, meta):
         target = lax.rem(me + off, n)
 
         def look(k, found):
@@ -150,16 +148,12 @@
             return first, second
 
         first, second = lax.fori_loop(0, pairs, look, (jnp.int32(-1), jnp.int32(-1)), unroll=8)
-        meta = jnp.zeros((META, BLK), jnp.float32)
         for slot, source in enumerate((first, second)):
             index = jnp.maximum(source, 0)
             ref[off, slot * BLK:(slot + 1) * BLK, :] = tl_ref[tile_s[index]]
-            entries = jnp.minimum(map_ref[pl.ds(index, 1), :], BLK)
-            entries = jnp.where(source >= 0, entries, BLK).astype(jnp.float32)
-            block = block_s[index].astype(jnp.float32)
-            meta = jnp.where(meta_row == slot, entries, meta)
-            meta = jnp.where(meta_row == CAP + slot, block, meta)
-        ref[off, payload:payload + META, :] = meta.astype(jnp.bfloat16)
+            entries = map_ref[pl.ds(index, 1), :]
+            places = jnp.where(entries < BLK, block_s[index] * BLK + entries, v_local)
+            meta[off, slot:slot + 1, :] = jnp.where(source >= 0, places, v_local)
 
     def slot_copy(off):
         return pltpu.make_async_remote_copy(
@@ -179,10 +173,21 @@
         odd = lax.rem(i, 2)
         return spread(odd * (n - 2 - i // 2) + (1 - odd) * (i // 2), n)
 
+    def meta_copy(off):
+        return pltpu.make_async_remote_copy(
+            src_ref=send_meta.at[off],
+            dst_ref=recv_meta.at[off],
+            send_sem=meta_send_sem,
+            recv_sem=meta_recv_sem.at[off],
+            device_id={"vocab": lax.rem(me + off, n)},
+            device_id_type=pl.DeviceIdType.MESH,
+        )
+
     def send_slot(i, carry):
         off = slot_order(i)
-        fill(off, send_ref)
+        fill(off, send_ref, send_meta)
         slot_copy(off).start()
+        meta_copy(off).start()
         return carry
 
     early = n // 3
@@ -222,19 +227,16 @@
     share(2, mass, jnp.broadcast_to(part_mass, (8, tokens)))
 
     lax.fori_loop(early, n - 1, send_slot, 0)
-    fill(0, recv_ref)
+    fill(0, recv_ref, recv_meta)
 
     mapped_ref[...] = jnp.zeros_like(mapped_ref)
-    entry = lax.broadcasted_iota(jnp.int32, (v_local, BLK), 0).astype(jnp.float32)
+    entry = lax.broadcasted_iota(jnp.int32, (v_local, BLK), 0)
 
     def join(off):
         probs_ref[...] = jnp.exp(recv_ref[off, 0:payload, :].astype(jnp.float32) - lse).astype(jnp.bfloat16)
-        meta = recv_ref[off, payload:payload + META, :].astype(jnp.float32)
         pickers = []
         for slot in range(CAP):
-            entries = meta[slot:slot + 1, :]
-            blocks = meta[CAP + slot:CAP + slot + 1, :]
-            places = jnp.where(entries < BLK, blocks * BLK + entries, float(v_local))
+            places = recv_meta[off, slot:slot + 1, :]
             pickers.append(jnp.where(entry == places, 1.0, 0.0).astype(jnp.bfloat16))
         picker = jnp.concatenate(pickers, axis=1)
         mapped_ref[...] += jnp.dot(picker, probs_ref[...], preferred_element_type=jnp.float32)
@@ -244,6 +246,7 @@
     def join_next(i, carry):
         off = slot_order(i)
         slot_copy(off).wait_recv()
+        meta_copy(off).wait_recv()
         join(off)
         return carry
 
@@ -327,6 +330,7 @@
         pltpu.make_async_copy(ref, ref, sem).wait()
 
     drained(send_ref.at[pl.ds(1, n - 1)], a2a_send_sem)
+    drained(send_meta.at[pl.ds(1, n - 1)], meta_send_sem)
     for which, gathered in enumerate((tstat, sstat, mass)):
         drained(gathered.at[pl.ds(1, n - 1)], small_send_sem.at[which])
     drained(p_send, c_send_sem)
@@ -343,7 +347,7 @@
     rows = d_full // n
     cut = rows // CUTS
     tiles = teacher_codes.shape[0] // BLK
-    slot_rows = CAP * BLK + META
+    slot_rows = CAP * BLK
     f32, bf16 = jnp.float32, jnp.bfloat16
     vmem = pl.BlockSpec(memory_space=pltpu.VMEM)
     smem = pl.BlockSpec(memory_space=pltpu.SMEM)
@@ -361,6 +365,8 @@
             pltpu.VMEM((CAP * BLK, tokens), bf16),
             pltpu.VMEM((n, slot_rows, tokens), bf16),
             pltpu.VMEM((n, slot_rows, tokens), bf16),
+            pltpu.VMEM((n, CAP, BLK), jnp.int32),
+            pltpu.VMEM((n, CAP, BLK), jnp.int32),
             pltpu.VMEM((3, 8, tokens), f32),
             pltpu.VMEM((n, 8, tokens), f32),
             pltpu.VMEM((n, 8, tokens), f32),
@@ -377,6 +383,8 @@
             pltpu.VMEM(((A - 1) * CUTS, cut + SCALE_ROWS, tokens), jnp.int16),
             dma((W_CHUNKS,)),
             dma,
+            dma,
+            dma((n,)),
             dma,
             dma((n,)),
             dma((3,)),

time: 59.7 us -> 58.9 us (0.987)
  Pallas kernels: 57.9 us -> 57.1 us
    pallas_call x1, Pallas kernels: 57.9 us -> 57.1 us  [per_device(): pl.pallas_call(functools.partial(kernel, n, A, B), out_shape=jax.ShapeDty...]
where the time goes in v4:
time: 58.9 us; the launch traced here: 58.7 us
  Pallas kernels  57.1 us (97%)
  other arithmetic  1.62 us (3%)
    pallas_call x1, Pallas kernels, per_device(): pl.pallas_call(functools.partial(kernel, n, A, B), out_shape=jax.ShapeDty...  57.1 us
    convert_element_type x1, other arithmetic, per_device(): return pl.pallas_call(functools.partial(kernel, n, A, B), out_shape=jax.S...  1.62 us

profile of v4, /device:TPU:0, one launch (start us, length us, event | category | flops | bytes accessed | tf_op | source)
XLA Modules:
  0.0 58.7 jit_solution(1513095394675878636)
XLA Ops:
  0.0 57.1 %shard_map.82 = f32[512,128]{1,0:T(8,128)} custom-call(s32[24]{0:T(128)} %tile_s.1, s32[24]{0:T(128)} %bitcast.1, s32[24]{0:T(128)} %block_s.1, bf16[128,8192]{1,0:T(8,128)(2,1)} %hidden_hbm.1, bf16[8192,512]{1,0:T(8,128)(2,1)} %w_hbm.1, bf16[1024,128]{1,0:T(8,128)(2,1)} %codes_ref.1, s32[32,128]{1,0:T(8,128)} %exps_ref.1, s32[24,128]{1,0:T(8,128)} %map_ref.1), custom_call_target="tpu_custom_call" | custom-call | tf_op jit(solution)/shard_map/pallas_call | solution.py:356
  57.1 1.6 %convert_element_type.3 = bf16[512,128]{1,0:T(8,128)(2,1)} convert(f32[512,128]{1,0:T(8,128)} %shard_map.82) | non-fusion elementwise | flops 65536 | bytes 393216 | tf_op jit(solution)/shard_map/convert_element_type | solution.py:405

commit v5 on v4

--- a/solution.py
+++ b/solution.py
@@ -32,7 +32,7 @@
     rows = values.shape[0]
     top = jnp.maximum(jnp.max(jnp.abs(values), axis=0, keepdims=True), TINY)
     level = jnp.ceil(8.0 * jnp.log2(top))
-    step = TOP_CODE / jnp.exp2(level * 0.125)
+    step = TOP_CODE * jnp.exp2(level * -0.125)
     codes = jnp.round(values * step).astype(jnp.int32)
     ref[0:rows, :] = codes.astype(jnp.int16)
     levels = jnp.broadcast_to(level, (SCALE_ROWS, values.shape[1])).astype(jnp.int32)
@@ -295,7 +295,7 @@
 
     def step(i, carry):
         for j in range(B):
-            p_send[i * B + j] = product(i, j, 1 - core)
+            encode(product(i, j, 1 - core), p_send.at[i * B + j])
             core_copy(i, j).start()
             if j >= 1:
                 pass_on(i, j - 1)
@@ -304,12 +304,12 @@
 
     def pass_on(i, j):
         core_copy(i, j).wait_recv()
-        encode(p_own[i * B + j] + rc[i * B + j], sb.at[i * (B - 1) + j])
+        encode(p_own[i * B + j] + decode(rc.at[i * B + j]), sb.at[i * (B - 1) + j])
         b_copy(i, j).start()
 
     def collected(i):
         core_copy(i, B - 1).wait_recv()
-        acc = p_own[i * B + B - 1] + rc[i * B + B - 1]
+        acc = p_own[i * B + B - 1] + decode(rc.at[i * B + B - 1])
         for j in range(B - 1):
             b_copy(i, j).wait_recv()
             acc += decode(rb.at[i * (B - 1) + j])
@@ -374,9 +374,9 @@
             pltpu.VMEM((v_local, tokens), f32),
             pltpu.VMEM((v_local, tokens), f32),
             pltpu.VMEM((v_local, tokens), bf16),
+            pltpu.VMEM((A * CUTS * B, cut + SCALE_ROWS, tokens), jnp.int16),
             pltpu.VMEM((A * CUTS * B, cut, tokens), f32),
-            pltpu.VMEM((A * CUTS * B, cut, tokens), f32),
-            pltpu.VMEM((A * CUTS * B, cut, tokens), f32),
+            pltpu.VMEM((A * CUTS * B, cut + SCALE_ROWS, tokens), jnp.int16),
             pltpu.VMEM((A * CUTS * (B - 1), cut + SCALE_ROWS, tokens), jnp.int16),
             pltpu.VMEM(((A - 1) * CUTS, cut + SCALE_ROWS, tokens), jnp.int16),
             pltpu.VMEM((A * CUTS * (B - 1), cut + SCALE_ROWS, tokens), jnp.int16),

time: 58.9 us -> 58.8 us (level)
  no operation moved by 1% of the time
where the time goes in v5:
time: 58.8 us; the launch traced here: 58.7 us
  Pallas kernels  57.1 us (97%)
  other arithmetic  1.62 us (3%)
    pallas_call x1, Pallas kernels, per_device(): pl.pallas_call(functools.partial(kernel, n, A, B), out_shape=jax.ShapeDty...  57.1 us
    convert_element_type x1, other arithmetic, per_device(): return pl.pallas_call(functools.partial(kernel, n, A, B), out_shape=jax.S...  1.62 us

profile of v5, /device:TPU:0, one launch (start us, length us, event | category | flops | bytes accessed | tf_op | source)
XLA Modules:
  0.0 58.7 jit_solution(9373006585789346504)
XLA Ops:
  0.0 57.1 %shard_map.82 = f32[512,128]{1,0:T(8,128)} custom-call(s32[24]{0:T(128)} %tile_s.1, s32[24]{0:T(128)} %bitcast.1, s32[24]{0:T(128)} %block_s.1, bf16[128,8192]{1,0:T(8,128)(2,1)} %hidden_hbm.1, bf16[8192,512]{1,0:T(8,128)(2,1)} %w_hbm.1, bf16[1024,128]{1,0:T(8,128)(2,1)} %codes_ref.1, s32[32,128]{1,0:T(8,128)} %exps_ref.1, s32[24,128]{1,0:T(8,128)} %map_ref.1), custom_call_target="tpu_custom_call" | custom-call | tf_op jit(solution)/shard_map/pallas_call | solution.py:356
  57.1 1.6 %convert_element_type.3 = bf16[512,128]{1,0:T(8,128)(2,1)} convert(f32[512,128]{1,0:T(8,128)} %shard_map.82) | non-fusion elementwise | flops 65536 | bytes 393216 | tf_op jit(solution)/shard_map/convert_element_type | solution.py:405
